TPU v7x, 32 devices: a whole 2x2x4 slice. The times are simulated.
32 devices in a mesh: dp: 32 (over z, y, x, core).
Axes of the slice: x: 2, y: 2, z: 4, core: 2. Of those that a mesh axis runs over, the one named last changes fastest.
Arguments:
- tokens: bfloat16 [32768, 1024], P('dp'), may hold values from -6 to 6
- cotangent: bfloat16 [32768, 1024], P('dp'), may hold values from -6 to 6
- seq_lengths: int32 [32, 4], P('dp'), may hold values from 1 to 512, 1024 in all within a row
- live_seqs: int32 [32], P('dp'), may hold values from 2 to 4
- qkv_weight: bfloat16 [1024, 3072], P('dp'), may hold values from -0.1875 to 0.1875
- qkv_bias: bfloat16 [3072], P('dp'), may hold values from -2 to 2
- out_weight: bfloat16 [1024, 1024], P('dp'), may hold values from -1 to 1
- out_bias: bfloat16 [1024], P('dp'), may hold values from -2 to 2
- up_weight: bfloat16 [1024, 4096], P('dp'), may hold values from -0.1875 to 0.1875
- up_bias: bfloat16 [4096], P('dp'), may hold values from -3 to 3
- down_weight: bfloat16 [4096, 1024], P('dp'), may hold values from -0.09375 to 0.09375
- down_bias: bfloat16 [1024], P('dp'), may hold values from -2 to 2
- attn_gain: bfloat16 [1024], P('dp'), may hold values from 0.5 to 1.5
- attn_shift: bfloat16 [1024], P('dp'), may hold values from -2 to 2
- mlp_gain: bfloat16 [1024], P('dp'), may hold values from 0.5 to 1.5
- mlp_shift: bfloat16 [1024], P('dp'), may hold values from -2 to 2
Outputs:
- mixed: bfloat16 [32768, 1024], P('dp')
- token_grad: float32 [32768, 1024], P('dp')
- qkv_weight_grad: float32 [1024, 3072], P('dp')
- qkv_bias_grad: float32 [3072], P('dp')
- out_weight_grad: float32 [1024, 1024], P('dp')
- out_bias_grad: float32 [1024], P('dp')
- up_weight_grad: float32 [1024, 4096], P('dp')
- up_bias_grad: float32 [4096], P('dp')
- down_weight_grad: float32 [4096, 1024], P('dp')
- down_bias_grad: float32 [1024], P('dp')
- attn_gain_grad: float32 [1024], P('dp')
- attn_shift_grad: float32 [1024], P('dp')
- mlp_gain_grad: float32 [1024], P('dp')
- mlp_shift_grad: float32 [1024], P('dp')
Inputs may be any that keep to these rules, and one draw needn't show every extreme that they name: `seq_lengths`: each row holds the lengths of one device's 4 sequences, which fill its 1024 slots exactly; every row has one sequence of exactly 512. A device's first live_seqs sequences are live, the rest are padding whose cotangent is dropped.
All inputs are finite; a program needn't handle non-finite values.
Results may differ from a plain program's by a relative error of at most 0.0095.
Values may be sent and summed in bfloat16 or wider, within the bound.
A program may use at most 256 MiB of HBM per device.

v0:
```python
from functools import partial

import jax
import jax.numpy as jnp
from jax import lax
from jax.sharding import PartitionSpec as P

D = 1024
HEADS = 16
HEAD = 64
ROT = 16
QBLOCK = 512


EPS = 1e-05
MASKED = -1e30


def layout(lengths, live_count, rows):
    ends = jnp.cumsum(lengths)
    starts = ends - lengths
    places = jnp.arange(rows, dtype=jnp.int32)
    segment = jnp.sum((places[:, None] >= ends[None, :]).astype(jnp.int32), axis=1)
    choose = segment[:, None] == jnp.arange(lengths.shape[0], dtype=jnp.int32)[None, :]
    offset = jnp.sum(jnp.where(choose, starts[None, :], 0), axis=1)
    live = (segment < live_count).astype(jnp.float32)
    return (segment, places - offset, live)


def rotary(positions):
    half = ROT // 2
    freqs = 10000.0 ** (-(2.0 * jnp.arange(half, dtype=jnp.float32)) / ROT)
    angles = positions.astype(jnp.float32)[:, None, None] * freqs[None, None, :]
    return (jnp.cos(angles), jnp.sin(angles))


def rotate(values, cosine, sine):
    half = ROT // 2
    first = values[..., :half]
    second = values[..., half:ROT]
    return jnp.concatenate(
        [first * cosine - second * sine, second * cosine + first * sine, values[..., ROT:]], axis=-1
    )


def normalize(inputs):
    average = jnp.mean(inputs, axis=1, keepdims=True)
    centred = inputs - average
    variance = jnp.mean(centred * centred, axis=1, keepdims=True)
    inverse = lax.rsqrt(variance + EPS)
    return (centred * inverse, inverse)


def outer_sum(left, right):
    return lax.dot_general(
        left, right, (((0,), (0,)), ((), ())), preferred_element_type=jnp.float32
    )


def times_transposed(left, right):
    return lax.dot_general(
        left, right, (((1,), (1,)), ((), ())), preferred_element_type=jnp.float32
    )


def block_scores(query, keys, segment, begin):
    places = jnp.arange(keys.shape[0], dtype=jnp.int32)
    block_query = lax.dynamic_slice_in_dim(query, begin, QBLOCK, 0)
    block_segment = lax.dynamic_slice_in_dim(segment, begin, QBLOCK, 0)
    block_places = begin + jnp.arange(QBLOCK, dtype=jnp.int32)
    allowed = (block_segment[:, None] == segment[None, :]) & (
        places[None, :] <= block_places[:, None]
    )
    scores = jnp.einsum(
        "qhd,khd->hqk", block_query, keys, preferred_element_type=jnp.float32
    ) * HEAD ** (-0.5)
    return (jnp.where(allowed[None], scores, MASKED), block_query)


def attention_forward(query, keys, values, segment):
    rows = query.shape[0]

    def one_block(index):
        masked, block_query = block_scores(query, keys, segment, index * QBLOCK)
        largest = jnp.max(masked, axis=-1, keepdims=True)
        weights = jnp.exp(masked - largest)
        totals = jnp.sum(weights, axis=-1, keepdims=True)
        probs = (weights / totals).astype(jnp.bfloat16)
        result = jnp.einsum("hqk,khd->qhd", probs, values, preferred_element_type=jnp.float32)
        return (result, largest + jnp.log(totals))

    results, logsums = lax.map(one_block, jnp.arange(rows // QBLOCK, dtype=jnp.int32))
    return (results.reshape(rows, D), logsums)


def attention_backward(query, keys, values, segment, logsums, grad_heads):
    rows = query.shape[0]
    scale = HEAD ** (-0.5)

    def one_block(carry, index):
        key_grad, value_grad = carry
        begin = index * QBLOCK
        masked, block_query = block_scores(query, keys, segment, begin)
        probs = jnp.exp(masked - logsums[index])
        block_grad = lax.dynamic_slice_in_dim(grad_heads, begin, QBLOCK, 0)
        prob_grad = jnp.einsum(
            "qhd,khd->hqk", block_grad, values, preferred_element_type=jnp.float32
        )
        inner = jnp.sum(probs * prob_grad, axis=-1, keepdims=True)
        score_grad = (probs * (prob_grad - inner)).astype(jnp.bfloat16)
        query_grad = (
            jnp.einsum("hqk,khd->qhd", score_grad, keys, preferred_element_type=jnp.float32) * scale
        )
        key_grad = (
            key_grad
            + jnp.einsum(
                "hqk,qhd->khd", score_grad, block_query, preferred_element_type=jnp.float32
            )
            * scale
        )
        value_grad = value_grad + jnp.einsum(
            "hqk,qhd->khd",
            probs.astype(jnp.bfloat16),
            block_grad,
            preferred_element_type=jnp.float32,
        )
        return ((key_grad, value_grad), query_grad)

    empty = jnp.zeros((rows, HEADS, HEAD), jnp.float32)
    (key_grad, value_grad), query_grads = lax.scan(
        one_block, (empty, empty), jnp.arange(rows // QBLOCK, dtype=jnp.int32)
    )
    return (query_grads.reshape(rows, HEADS, HEAD), key_grad, value_grad)


def per_device(
    tokens,
    cotangent,
    seq_lengths,
    live_seqs,
    qkv_weight,
    qkv_bias,
    out_weight,
    out_bias,
    up_weight,
    up_bias,
    down_weight,
    down_bias,
    attn_gain,
    attn_shift,
    mlp_gain,
    mlp_shift,
):
    rows = tokens.shape[0]
    segment, positions, live = layout(seq_lengths[0], live_seqs[0], rows)
    shared = (
        lax.all_gather(qkv_bias, "dp", axis=0, tiled=True),
        lax.all_gather(up_bias, "dp", axis=0, tiled=True),
        lax.all_gather(out_bias, "dp", axis=0, tiled=True),
        lax.all_gather(down_bias, "dp", axis=0, tiled=True),
        lax.all_gather(attn_gain, "dp", axis=0, tiled=True),
        lax.all_gather(attn_shift, "dp", axis=0, tiled=True),
        lax.all_gather(mlp_gain, "dp", axis=0, tiled=True),
        lax.all_gather(mlp_shift, "dp", axis=0, tiled=True),
    )
    (
        joined_bias,
        hidden_bias,
        attn_bias,
        mlp_bias,
        attn_scale,
        attn_offset,
        mlp_scale,
        mlp_offset,
    ) = [member.astype(jnp.float32) for member in shared]
    inputs = tokens.astype(jnp.float32)
    normed, inverse = normalize(inputs)
    attn_in = (normed * attn_scale + attn_offset).astype(jnp.bfloat16)
    mlp_in = (normed * mlp_scale + mlp_offset).astype(jnp.bfloat16)
    local_rows = out_weight.shape[0]
    ratio = down_weight.shape[0] // local_rows
    down_view = down_weight.reshape(local_rows, ratio * D)
    pieces = (
        lax.all_gather(qkv_weight, "dp", axis=0, tiled=True),
        lax.all_gather(up_weight, "dp", axis=0, tiled=True),
    )
    left_attn = attn_in
    joined = jnp.dot(left_attn, pieces[0], preferred_element_type=jnp.float32)
    hidden_pre = jnp.dot(mlp_in, pieces[1], preferred_element_type=jnp.float32)
    joined = joined + joined_bias
    hidden_pre = hidden_pre + hidden_bias
    cosine, sine = rotary(positions)
    query = rotate(joined[:, :D].reshape(rows, HEADS, HEAD), cosine, sine).astype(jnp.bfloat16)
    keys = rotate(joined[:, D : 2 * D].reshape(rows, HEADS, HEAD), cosine, sine).astype(
        jnp.bfloat16
    )
    values = joined[:, 2 * D :].reshape(rows, HEADS, HEAD).astype(jnp.bfloat16)
    heads_out, logsums = attention_forward(query, keys, values, segment)
    attended = heads_out.astype(jnp.bfloat16)
    hidden = jax.nn.gelu(hidden_pre, approximate=False).astype(jnp.bfloat16)
    pieces = (
        lax.all_gather(out_weight, "dp", axis=0, tiled=True),
        lax.all_gather(down_view, "dp", axis=0, tiled=True),
    )
    count = pieces[0].shape[0]
    left_attn = attended
    rows_down = pieces[1].reshape(count * ratio, D)
    branches = jnp.dot(left_attn, pieces[0], preferred_element_type=jnp.float32) + jnp.dot(
        hidden, rows_down, preferred_element_type=jnp.float32
    )
    mixed = (inputs + branches + attn_bias + mlp_bias).astype(jnp.bfloat16)
    out_grad = cotangent.astype(jnp.float32) * live[:, None]
    out_low = out_grad.astype(jnp.bfloat16)
    bias_grad = jnp.sum(out_grad, axis=0)
    out_weight_grad = outer_sum(attended, out_low)
    down_weight_grad = outer_sum(hidden, out_low)
    pieces = lax.all_gather((out_weight, down_view), "dp", axis=0, tiled=True)
    count = pieces[0].shape[0]
    rows_down = pieces[1].reshape(count * ratio, D)
    attended_grad = times_transposed(out_low, pieces[0])
    hidden_grad = times_transposed(out_low, rows_down)
    attended_low = attended_grad.astype(jnp.bfloat16).reshape(rows, HEADS, HEAD)
    _, gelu_back = jax.vjp(partial(jax.nn.gelu, approximate=False), hidden_pre)
    pre_grad = gelu_back(hidden_grad)[0].astype(jnp.bfloat16)
    query_grad, key_grad, value_grad = attention_backward(
        query, keys, values, segment, logsums, attended_low
    )
    query_grad = rotate(query_grad, cosine, -sine)
    key_grad = rotate(key_grad, cosine, -sine)
    joined_grad = jnp.concatenate(
        [query_grad.reshape(rows, D), key_grad.reshape(rows, D), value_grad.reshape(rows, D)],
        axis=1,
    ).astype(jnp.bfloat16)
    joined_weight_grad = outer_sum(attn_in, joined_grad)
    up_weight_grad = outer_sum(mlp_in, pre_grad)
    joined_bias_grad = jnp.sum(joined_grad.astype(jnp.float32), axis=0)
    hidden_bias_grad = jnp.sum(pre_grad.astype(jnp.float32), axis=0)
    pieces = lax.all_gather((qkv_weight, up_weight), "dp", axis=0, tiled=True)
    attn_in_grad = times_transposed(joined_grad, pieces[0])
    mlp_in_grad = times_transposed(pre_grad, pieces[1])
    attn_scale_grad = jnp.sum(attn_in_grad * normed, axis=0)
    attn_offset_grad = jnp.sum(attn_in_grad, axis=0)
    mlp_scale_grad = jnp.sum(mlp_in_grad * normed, axis=0)
    mlp_offset_grad = jnp.sum(mlp_in_grad, axis=0)
    normed_grad = attn_in_grad * attn_scale + mlp_in_grad * mlp_scale
    token_grad = (
        inverse
        * (
            normed_grad
            - jnp.mean(normed_grad, axis=1, keepdims=True)
            - normed * jnp.mean(normed_grad * normed, axis=1, keepdims=True)
        )
        + out_grad
    )
    everything = (
        lax.psum_scatter(joined_weight_grad, "dp", scatter_dimension=0, tiled=True),
        lax.psum_scatter(up_weight_grad, "dp", scatter_dimension=0, tiled=True),
        lax.psum_scatter(joined_bias_grad, "dp", scatter_dimension=0, tiled=True),
        lax.psum_scatter(hidden_bias_grad, "dp", scatter_dimension=0, tiled=True),
        lax.psum_scatter(attn_scale_grad, "dp", scatter_dimension=0, tiled=True),
        lax.psum_scatter(attn_offset_grad, "dp", scatter_dimension=0, tiled=True),
        lax.psum_scatter(mlp_scale_grad, "dp", scatter_dimension=0, tiled=True),
        lax.psum_scatter(mlp_offset_grad, "dp", scatter_dimension=0, tiled=True),
        lax.psum_scatter(out_weight_grad, "dp", scatter_dimension=0, tiled=True),
        lax.psum_scatter(down_weight_grad, "dp", scatter_dimension=0, tiled=True),
        lax.psum_scatter(bias_grad, "dp", scatter_dimension=0, tiled=True),
    )
    summed = everything[:8]
    owned_out, owned_down, owned_bias = (everything[8], everything[9], everything[10])
    return (
        mixed,
        token_grad,
        summed[0],
        summed[2],
        owned_out,
        owned_bias,
        summed[1],
        summed[3],
        owned_down,
        owned_bias,
        summed[4],
        summed[5],
        summed[6],
        summed[7],
    )


def solution(mesh):
    return jax.shard_map(
        per_device,
        mesh=mesh,
        in_specs=(
            P("dp", None),
            P("dp", None),
            P("dp", None),
            P("dp"),
            P("dp", None),
            P("dp"),
            P("dp", None),
            P("dp"),
            P("dp", None),
            P("dp"),
            P("dp", None),
            P("dp"),
            P("dp"),
            P("dp"),
            P("dp"),
            P("dp"),
        ),
        out_specs=(
            P("dp", None),
            P("dp", None),
            P("dp", None),
            P("dp"),
            P("dp", None),
            P("dp"),
            P("dp", None),
            P("dp"),
            P("dp", None),
            P("dp"),
            P("dp"),
            P("dp"),
            P("dp"),
            P("dp"),
        ),
        check_vma=False,
    )
```

profile of v0, /device:TPU:0, one launch (start us, length us, event | category | flops | bytes accessed | tf_op | source)
XLA Modules:
  0.0 1158.5 jit_solution(3211613620642056592)
XLA Ops:
  8.7 1.8 reshape.336
  11.3 0.8 dynamic-update-slice
  16.3 0.8 dynamic-update-slice.2
  17.2 42.4 %all-reduce.15 = (bf16[3072]{0:T(1024)(128)(2,1)S(1)}, bf16[1024]{0:T(1024)(128)(2,1)S(1)}, bf16[1024]{0:T(1024)(128)(2,1)S(1)}, bf16[1024]{0:T(1024)(128)(2,1)}...) all-reduce(bf16[3072]{0:T(1024)(128)(2,1)S(1)} %dynamic-update-slic, ...), channel_id=1, replica_groups=mesh['dp'=32] {'dp'}, use_global_device_ids=true, to_apply=%add.2 | all-reduce | flops 9216 | bytes 36864
  59.6 1.9 convert_reduce_fusion.2
  64.5 41.0 %all-gather = bf16[32,1,128]{2,1,0:T(2,128)(2,1)S(1)} all-gather(bf16[1,1,128]{2,1,0:T(2,128)(2,1)S(1)} %bitcast.115), channel_id=1, replica_groups=mesh['dp'=32] {'dp'}, dimensions={0}, use_global_device_ids=true | all-gather | bytes 8448 | tf_op jit(solution)/shard_map/all_gather | solution.py:158
  106.9 6.0 convolution_convert_fusion
  113.0 28.5 %all-gather.6.cloned.1.call-done = bf16[1024,3072]{1,0:T(8,128)(2,1)} async-done(((bf16[32,3072]{1,0:T(8,128)(2,1)}), bf16[1024,3072]{1,0:T(8,128)(2,1)}) %all-gather.6.cloned.1.call-update) | async-done | bytes 6291472 | tf_op jit(solution)/shard_map/all_gather | solution.py:184
  141.5 9.0 broadcast_add_fusion
  150.5 4.2 fusion.81
  155.0 5.4 copy.48
  160.4 5.4 copy.49
  165.8 3.3 slice.102
  169.1 3.5 slice.103
  172.6 2.6 copy.50
  175.2 2.0 subtract_convert_fusion.2
  177.7 1.5 pad_maximum_fusion.1
  179.2 98.4 %while.27 = (s32[]{:T(128)}, bf16[2,512,16,64]{1,3,2,0:T(8,128)(2,1)}, f32[2,16,512,1]{2,1,3,0:T(8,128)S(1)}, s32[2]{0:T(128)S(1)}, s32[1024]{0:T(1024)S(1)}, /*...) while((s32[]{:T(128)}, ...), condition=%wide.region_8.9_spmd, body=%wide.region_5.8_spmd.sunk | while | flops 2249712128 | bytes 118766296 | solution.py:92
  181.7 16.3 %fusion.123 = (f32[16,512]{1,0:T(8,128)S(1)}, f32[16,512,1024]{2,1,0:T(8,128)}) fusion(pred[512,1024]{1,0:T(8,128)(4,1)S(1)} %fusion.122, bf16[1024,16,64]{0,2,1:T(8,128)(2,1)S(1)} %get-tuple-element.424, bf16[1024,16,64]{0,2,1:T(8,128)(2,1)} %get-tuple-element.423, s32[]{:T(128)S(6)} %select_n.62), kind=kOutput, calls=%fused_computation.3.clone.1 | convolution fusion | flops 1098899456 | bytes 37257220 | tf_op jit(solution)/shard_map/while/body/eval_jaxpr/qhd,khd->hqk/dot_general | solution.py:74
  198.0 15.2 %fusion.124 = f32[16,512]{1,0:T(8,128)S(1)} fusion(f32[16,512,1024]{2,1,0:T(8,128)} %get-tuple-element.379, f32[16,512]{1,0:T(8,128)S(1)} %get-tuple-element.380, pred[512,1024]{1,0:T(8,128)(4,1)S(1)} %fusion.122), kind=kLoop, calls=%fused_computation.4.clone.1 | loop fusion | flops 33546240 | bytes 34144256 | tf_op jit(solution)/shard_map/while/body/eval_jaxpr/reduce_sum | solution.py:87
  213.3 15.4 %bitcast_dynamic-update-slice_fusion.4 = bf16[2,512,16,64]{1,3,2,0:T(8,128)(2,1)} fusion(bf16[2,512,16,64]{1,3,2,0:T(8,128)(2,1)} %get-tuple-element.407, s32[]{:T(128)} %get-tuple-element.406, bf16[1024,16,64]{0,2,1:T(8,128)(2,1)S(1)} %copy-done, f32[16,512,1024]{2,1,0:T(8,128)} %get-tuple-element.379, f32[16,512]{1,0:T(8,128)S(1)} %fusion.124, ...), kind=kOutput, calls=%fused_computation.6.clone.1 | convolution fusion | flops 1115684864 | bytes 38339072 | tf_op jit(solution)/shard_map/while/body/eval_jaxpr/hqk,khd->qhd/dot_general | solution.py:89
  230.7 15.4 %fusion.123 = (f32[16,512]{1,0:T(8,128)S(1)}, f32[16,512,1024]{2,1,0:T(8,128)}) fusion(pred[512,1024]{1,0:T(8,128)(4,1)S(1)} %fusion.122, bf16[1024,16,64]{0,2,1:T(8,128)(2,1)S(1)} %get-tuple-element.424, bf16[1024,16,64]{0,2,1:T(8,128)(2,1)} %get-tuple-element.423, s32[]{:T(128)S(6)} %select_n.62), kind=kOutput, calls=%fused_computation.3.clone.1 | convolution fusion | flops 1098899456 | bytes 37257220 | tf_op jit(solution)/shard_map/while/body/eval_jaxpr/qhd,khd->hqk/dot_general | solution.py:74
  246.0 15.2 %fusion.124 = f32[16,512]{1,0:T(8,128)S(1)} fusion(f32[16,512,1024]{2,1,0:T(8,128)} %get-tuple-element.379, f32[16,512]{1,0:T(8,128)S(1)} %get-tuple-element.380, pred[512,1024]{1,0:T(8,128)(4,1)S(1)} %fusion.122), kind=kLoop, calls=%fused_computation.4.clone.1 | loop fusion | flops 33546240 | bytes 34144256 | tf_op jit(solution)/shard_map/while/body/eval_jaxpr/reduce_sum | solution.py:87
  261.3 16.3 %bitcast_dynamic-update-slice_fusion.4 = bf16[2,512,16,64]{1,3,2,0:T(8,128)(2,1)} fusion(bf16[2,512,16,64]{1,3,2,0:T(8,128)(2,1)} %get-tuple-element.407, s32[]{:T(128)} %get-tuple-element.406, bf16[1024,16,64]{0,2,1:T(8,128)(2,1)S(1)} %copy-done, f32[16,512,1024]{2,1,0:T(8,128)} %get-tuple-element.379, f32[16,512]{1,0:T(8,128)S(1)} %fusion.124, ...), kind=kOutput, calls=%fused_computation.6.clone.1 | convolution fusion | flops 1115684864 | bytes 38339072 | tf_op jit(solution)/shard_map/while/body/eval_jaxpr/hqk,khd->qhd/dot_general | solution.py:89
  277.6 3.9 copy.51
  282.1 1.3 copy-done.12
  283.4 4.5 fusion.70
  288.0 306.0 %while.28 = (s32[]{:T(128)}, f32[1024,16,64]{0,2,1:T(8,128)}, f32[1024,16,64]{0,2,1:T(8,128)}, f32[2,512,16,64]{1,0,3,2:T(2,128)}, s32[2]{0:T(128)S(1)}, /*index...) while((s32[]{:T(128)}, f32[1024,16,64]{0,2,1:T(8,128)}, ...), condition=%wide.region_11.12_spmd.clone, body=%wide.region_9.11_spmd.clone.sunk | while | flops 5501870592 | bytes 291748096 | solution.py:130
  290.1 14.8 %fusion.134 = f32[16,512,1024]{2,1,0:T(8,128)} fusion(bf16[1024,16,64]{0,2,1:T(8,128)(2,1)S(1)} %get-tuple-element.469, bf16[1024,16,64]{0,2,1:T(8,128)(2,1)} %get-tuple-element.467, s32[]{:T(128)S(6)} %select_n.66), kind=kOutput, calls=%fused_computation.31.clone.1 | convolution fusion | flops 1073741824 | bytes 36700164 | tf_op jit(solution)/shard_map/while/body/eval_jaxpr/qhd,khd->hqk/dot_general | solution.py:74
  306.8 25.9 %multiply_reduce_fusion.2 = (f32[16,512]{1,0:T(8,128)S(1)}, f32[16,512,1024]{2,1,0:T(8,128)}) fusion(f32[16,512,1024]{2,1,0:T(8,128)} %fusion.134, f32[16,512]{1,0:T(8,128)S(1)} %dynamic-slice_bitcast_fusion.2, pred[512,1024]{1,0:T(8,128)(4,1)S(1)} %fusion.135, bf16[1024,16,64]{0,2,1:T(8,128)(2,1)} %get-tuple-element.472, ...), kind=kOutput, calls=%fused_computation.17.clone.1 | convolution fusion | flops 1115676672 | bytes 70844416 | tf_op jit(solution)/shard_map/while/body/eval_jaxpr/qhd,khd->hqk/dot_general | solution.py:106
  332.8 28.1 %multiply_convert_fusion.3 = bf16[16,512,1024]{2,1,0:T(8,128)(2,1)} fusion(f32[16,512,1024]{2,1,0:T(8,128)} %get-tuple-element.392, f32[16,512,1024]{2,1,0:T(8,128)} %fusion.134, f32[16,512]{1,0:T(8,128)S(1)} %get-tuple-element.393, f32[16,512]{1,0:T(8,128)S(1)} %dynamic-slice_bitcast_fusion.2, pred[512,1024]{1,0:T(8,128)(4,1)S(1)} %fusion.135), kind=kLoop, calls=%fused_computation.16.clone.1 | loop fusion | flops 50331648 | bytes 84475904 | tf_op jit(solution)/shard_map/while/body/eval_jaxpr/convert_element_type | solution.py:110
  360.9 8.7 multiply_bitcast_fusion.2
  369.6 3.5 copy.68
  373.1 38.2 %dynamic_update_slice.19 = f32[2,512,16,64]{1,0,3,2:T(2,128)} dynamic-update-slice(f32[2,512,16,64]{1,0,3,2:T(2,128)} %get-tuple-element.449, f32[1,512,16,64]{1,0,3,2:T(1,128)} %copy.68, s32[]{:T(128)} %get-tuple-element.446, s32[]{:T(128)} %constant.72.clone.1..sunk.1, s32[]{:T(128)} %constant.72.clone.1..sunk.1, s32[]{:T(128)} %constant.72.clone.1..sunk.1) | dynamic-update-slice | bytes 4194308 | tf_op jit(solution)/shard_map/while/body/jit(dynamic_update_index_in_dim)/dynamic_update_slice | solution.py:92
  411.3 11.3 bitcast_add_fusion.4
  422.5 17.6 %bitcast_add_fusion.5 = f32[1024,16,64]{0,2,1:T(8,128)} fusion(f32[1024,16,64]{0,2,1:T(8,128)} %get-tuple-element.448, f32[16,512,1024]{2,1,0:T(8,128)} %fusion.134, f32[16,512]{1,0:T(8,128)S(1)} %dynamic-slice_bitcast_fusion.2, pred[512,1024]{1,0:T(8,128)(4,1)S(1)} %fusion.135, pred[]{:T(512)S(6)} %compare.3, ...), kind=kOutput, calls=%fused_computation.22.clone.1 | convolution fusion | flops 1109393408 | bytes 43548676 | tf_op jit(solution)/shard_map/while/body/eval_jaxpr/hqk,qhd->khd/dot_general | solution.py:121
  442.0 14.4 %fusion.134 = f32[16,512,1024]{2,1,0:T(8,128)} fusion(bf16[1024,16,64]{0,2,1:T(8,128)(2,1)S(1)} %get-tuple-element.469, bf16[1024,16,64]{0,2,1:T(8,128)(2,1)} %get-tuple-element.467, s32[]{:T(128)S(6)} %select_n.66), kind=kOutput, calls=%fused_computation.31.clone.1 | convolution fusion | flops 1073741824 | bytes 36700164 | tf_op jit(solution)/shard_map/while/body/eval_jaxpr/qhd,khd->hqk/dot_general | solution.py:74
  458.4 25.9 %multiply_reduce_fusion.2 = (f32[16,512]{1,0:T(8,128)S(1)}, f32[16,512,1024]{2,1,0:T(8,128)}) fusion(f32[16,512,1024]{2,1,0:T(8,128)} %fusion.134, f32[16,512]{1,0:T(8,128)S(1)} %dynamic-slice_bitcast_fusion.2, pred[512,1024]{1,0:T(8,128)(4,1)S(1)} %fusion.135, bf16[1024,16,64]{0,2,1:T(8,128)(2,1)} %get-tuple-element.472, ...), kind=kOutput, calls=%fused_computation.17.clone.1 | convolution fusion | flops 1115676672 | bytes 70844416 | tf_op jit(solution)/shard_map/while/body/eval_jaxpr/qhd,khd->hqk/dot_general | solution.py:106
  484.3 27.7 %multiply_convert_fusion.3 = bf16[16,512,1024]{2,1,0:T(8,128)(2,1)} fusion(f32[16,512,1024]{2,1,0:T(8,128)} %get-tuple-element.392, f32[16,512,1024]{2,1,0:T(8,128)} %fusion.134, f32[16,512]{1,0:T(8,128)S(1)} %get-tuple-element.393, f32[16,512]{1,0:T(8,128)S(1)} %dynamic-slice_bitcast_fusion.2, pred[512,1024]{1,0:T(8,128)(4,1)S(1)} %fusion.135), kind=kLoop, calls=%fused_computation.16.clone.1 | loop fusion | flops 50331648 | bytes 84475904 | tf_op jit(solution)/shard_map/while/body/eval_jaxpr/convert_element_type | solution.py:110
  512.1 8.7 multiply_bitcast_fusion.2
  520.8 3.5 copy.68
  524.3 38.1 %dynamic_update_slice.19 = f32[2,512,16,64]{1,0,3,2:T(2,128)} dynamic-update-slice(f32[2,512,16,64]{1,0,3,2:T(2,128)} %get-tuple-element.449, f32[1,512,16,64]{1,0,3,2:T(1,128)} %copy.68, s32[]{:T(128)} %get-tuple-element.446, s32[]{:T(128)} %constant.72.clone.1..sunk.1, s32[]{:T(128)} %constant.72.clone.1..sunk.1, s32[]{:T(128)} %constant.72.clone.1..sunk.1) | dynamic-update-slice | bytes 4194308 | tf_op jit(solution)/shard_map/while/body/jit(dynamic_update_index_in_dim)/dynamic_update_slice | solution.py:92
  562.4 12.4 %bitcast_add_fusion.4 = f32[1024,16,64]{0,2,1:T(8,128)} fusion(f32[1024,16,64]{0,2,1:T(8,128)} %get-tuple-element.447, bf16[16,512,1024]{2,1,0:T(8,128)(2,1)} %multiply_convert_fusion.3, pred[]{:T(512)S(6)} %compare.3, bf16[1024,16,64]{0,2,1:T(8,128)(2,1)} %get-tuple-element.467, s32[]{:T(128)S(6)} %select_n.66), kind=kOutput, calls=%fused_computation.23.clone.1 | convolution fusion | flops 1076887552 | bytes 26214404 | tf_op jit(solution)/shard_map/while/body/eval_jaxpr/hqk,qhd->khd/dot_general | solution.py:116
  574.9 18.8 %bitcast_add_fusion.5 = f32[1024,16,64]{0,2,1:T(8,128)} fusion(f32[1024,16,64]{0,2,1:T(8,128)} %get-tuple-element.448, f32[16,512,1024]{2,1,0:T(8,128)} %fusion.134, f32[16,512]{1,0:T(8,128)S(1)} %dynamic-slice_bitcast_fusion.2, pred[512,1024]{1,0:T(8,128)(4,1)S(1)} %fusion.135, pred[]{:T(512)S(6)} %compare.3, ...), kind=kOutput, calls=%fused_computation.22.clone.1 | convolution fusion | flops 1109393408 | bytes 43548676 | tf_op jit(solution)/shard_map/while/body/eval_jaxpr/hqk,qhd->khd/dot_general | solution.py:121
  594.0 6.6 reshape.339
  600.7 2.3 slice.101
  603.0 2.1 slice.100
  605.5 2.5 subtract_convert_fusion.1
  608.6 1.1 copy-done.5
  610.5 11.7 %fusion.64 = f32[1024,3072]{1,0:T(8,128)} fusion(bf16[1024,1024]{1,0:T(8,128)(2,1)S(1)} %copy-done.2, f32[1024]{0:T(1024)S(1)} %copy-done.33, f32[1024]{0:T(1024)S(1)} %copy-done.28, f32[1024]{0:T(1024)S(1)} %copy-done.22, f32[1024]{0:T(1024)S(1)} %copy-done.20, bf16[1024,1024]{0,1:T(8,128)(2,1)S(1)} %bitcast.101, bf16[1024,1024]{0,1:T(8,128)(2,1)S(1)} %bitcast.107, ...), kind=kOutput, calls=%fused_computation.127 | convolution fusion | flops 6467616768 | bytes 20987904 | tf_op jit(solution)/shard_map/dot_general | solution.py:55
  622.3 14.4 %reshape.337 = bf16[4096,1024]{1,0:T(8,128)(2,1)} reshape(bf16[1024,4096]{1,0:T(8,128)(2,1)} %all-gather.12.cloned.1.call-done) | data formatting | bytes 16777216 | tf_op jit(solution)/shard_map/reshape | solution.py:207
  636.7 51.3 %multiply_convert_fusion.1 = (bf16[1024,4096]{1,0:T(8,128)(2,1)}, f32[1024,4096]{1,0:T(8,128)}, f32[1024,4096]{1,0:T(8,128)}) fusion(f32[4096]{0:T(1024)S(1)} %bitcast.113, bf16[1024,4096]{1,0:T(8,128)(2,1)} %all-gather.10.cloned.1.call-done, bf16[1024,1024]{1,0:T(8,128)(2,1)S(1)} %copy-done.2, f32[1024]{0:T(1024)S(1)} %copy-done.31, ...), kind=kOutput, calls=%fused_computation.45 | convolution fusion | flops 8873050112 | bytes 52461568 | tf_op jit(solution)/shard_map/dot_general | solution.py:189
  688.0 24.5 %convert_reduce_fusion = (f32[4096]{0:T(1024)S(1)}, bf16[1024,4096]{1,0:T(8,128)(2,1)}) fusion(f32[1024,4096]{1,0:T(8,128)} %get-tuple-element.236, bf16[4096,1024]{1,0:T(8,128)(2,1)} %reshape.337, bf16[1024,1024]{1,0:T(8,128)(2,1)} %param.21, f32[1024]{0:T(1024)S(1)} %copy-done.25, f32[1024,4096]{1,0:T(8,128)} %get-tuple-element.265, f32[4096]{0:T(1024)S(1)} %bitcast.114), kind=kOutput, calls=%fused_computation.43 | convolution fusion | flops 8664379392 | bytes 52465664 | tf_op jit(solution)/shard_map/dot_general | solution.py:61
  712.5 15.3 %fusion.60 = f32[1024,4096]{1,0:T(8,128)} fusion(bf16[1024,4096]{1,0:T(8,128)(2,1)} %get-tuple-element.267, bf16[1024,1024]{1,0:T(8,128)(2,1)S(1)} %copy-done.2, f32[1024]{0:T(1024)S(1)} %copy-done.31, f32[1024]{0:T(1024)S(1)} %copy-done.30, f32[1024]{0:T(1024)S(1)} %copy-done.22, f32[1024]{0:T(1024)S(1)} %copy-done.20), kind=kOutput, calls=%fused_computation.125 | convolution fusion | flops 8596226048 | bytes 27279360 | tf_op jit(solution)/shard_map/dot_general | solution.py:55
  727.8 16.4 %fusion.68 = f32[4096,1024]{1,0:T(8,128)} fusion(bf16[1024,4096]{1,0:T(8,128)(2,1)} %get-tuple-element.235, bf16[1024,1024]{1,0:T(8,128)(2,1)} %param.21, f32[1024]{0:T(1024)S(1)} %copy-done.25), kind=kOutput, calls=%fused_computation.129 | convolution fusion | flops 8593080320 | bytes 27267072 | tf_op jit(solution)/shard_map/dot_general | solution.py:55
  744.9 5.2 convert_reduce_fusion.1
  750.2 4.4 fusion.82
  754.6 9.6 fusion.67
  764.2 15.5 %fusion.77 = (f32[1024]{0:T(1024)S(1)}, f32[1024]{0:T(1024)S(1)}, f32[1024]{0:T(1024)S(1)}, f32[1024]{0:T(1024)S(1)}, f32[1024,1024]{1,0:T(8,128)S(1)}, /*index=5*/f32[1024]{0:T(1024)S(1)}, f32[1024]{0:T(1024)S(1)}) fusion(f32[1024]{0:T(1024)S(1)} %copy-done.22, f32[1024]{0:T(1024)S(1)} %copy-done.20, bf16[1024,1024]{1,0:T(8,128)(2,1)S(1)} %copy-done.2, ...), kind=kOutput, calls=%fused_computation.132 | convolution fusion | flops 8605657088 | bytes 27303936 | tf_op jit(solution)/shard_map/dot_general | solution.py:61
  779.8 3.4 fusion.56
  783.2 47.0 %all-reduce.14 = (f32[3072]{0:T(1024)S(1)}, f32[1024]{0:T(1024)S(1)}, f32[4096]{0:T(1024)S(1)}, f32[1024]{0:T(1024)S(1)}, f32[1024]{0:T(1024)S(1)}, /*index=5*/f32[1024]{0:T(1024)S(1)}, f32[1024]{0:T(1024)S(1)}) all-reduce(f32[3072]{0:T(1024)S(1)} %convert_reduce_fusion.1, ...), channel_id=3, replica_groups=mesh['dp'=32] {'dp'}, use_global_device_ids=true, to_apply=%region_16.17.clone | all-reduce | flops 12288 | bytes 98304
  833.8 15.7 %fusion.55 = bf16[1024,1024]{1,0:T(8,128)(2,1)} fusion(bf16[1024,1024]{1,0:T(8,128)(2,1)S(1)} %copy-done.2, f32[1024,1024]{1,0:T(8,128)} %fusion.82, f32[1024]{0:T(1024)S(1)} %convert_element_type.112, f32[1024]{0:T(1024)S(1)} %convert_element_type.111, bf16[1024,4096]{1,0:T(8,128)(2,1)} %get-tuple-element.235, bf16[4096,1024]{1,0:T(8,128)(2,1)} %reshape.337), kind=kOutput, calls=%fused_computation.86 | convolution fusion | flops 8596226048 | bytes 25174016 | tf_op jit(solution)/shard_map/dot_general | solution.py:208
  849.4 113.8 %reduce-scatter.9.cloned.1.call-done = f32[32,4096]{1,0:T(8,128)} async-done(((f32[1024,4096]{1,0:T(8,128)}), f32[32,4096]{1,0:T(8,128)}) %reduce-scatter.9.cloned.1.call-update) | async-done | bytes 524304 | tf_op jit(solution)/shard_map/reduce_scatter | solution.py:257
  963.2 187.8 %reduce-scatter.11.cloned.1.call-done = f32[128,1024]{1,0:T(8,128)} async-done(((f32[4096,1024]{1,0:T(8,128)}), f32[128,1024]{1,0:T(8,128)}) %reduce-scatter.11.cloned.1.call-update) | async-done | bytes 524304 | tf_op jit(solution)/shard_map/reduce_scatter | solution.py:265
  (174 shorter events, 23.2 us)
Async XLA Ops:
  7.2 54.4 %copy-start.1 = (bf16[1024,1024]{1,0:T(8,128)(2,1)S(1)}, bf16[1024,1024]{1,0:T(8,128)(2,1)}, u32[]{:S(2)}) copy-start(bf16[1024,1024]{1,0:T(8,128)(2,1)} %param.20) | copy-start | bytes 6291460
  7.2 55.1 %copy-start.38 = (s32[1,4]{1,0:T(1,128)S(1)}, s32[1,4]{1,0:T(1,128)}, u32[]{:S(2)}) copy-start(s32[1,4]{1,0:T(1,128)} %param.22) | copy-start | bytes 52
  7.2 57.3 %copy-start.36 = (bf16[128]{0:T(256)(128)(2,1)S(1)}, bf16[128]{0:T(256)(128)(2,1)}, u32[]{:S(2)}) copy-start(bf16[128]{0:T(256)(128)(2,1)} %param.29) | copy-start | bytes 772
  7.2 99.7 %all-gather.8.cloned.1.call-start = ((), (), s32[]{:S(2)}) async-start(), calls=%async_computation.5 | async-start | bytes 2162688 | tf_op jit(solution)/shard_map/all_gather | solution.py:202
  7.9 133.5 %all-gather.6.cloned.1.call-start = ((), (), s32[]{:S(2)}) async-start(), calls=%async_computation.4 | async-start | bytes 6488064 | tf_op jit(solution)/shard_map/all_gather | solution.py:184
  8.7 613.6 %all-gather.12.cloned.1.call-start = ((), (), s32[]{:S(2)}) async-start(), calls=%async_computation.7 | async-start | bytes 8650752 | tf_op jit(solution)/shard_map/all_gather | solution.py:203
  10.6 626.1 %all-gather.10.cloned.1.call-start = ((), (), s32[]{:S(2)}) async-start(), calls=%async_computation.6 | async-start | bytes 8650752 | tf_op jit(solution)/shard_map/all_gather | solution.py:185
  11.2 838.3 %reduce-scatter.7.cloned.1.call-start = ((), (), s32[]{:S(2)}) async-start(), calls=%async_computation.9 | async-start | bytes 4325376 | tf_op jit(solution)/shard_map/reduce_scatter | solution.py:264
  59.5 81.9 %copy-start.27 = (f32[1024]{0:T(1024)}, f32[1024]{0:T(1024)S(1)}, u32[]{:S(2)}) copy-start(f32[1024]{0:T(1024)S(1)} %convert_element_type.98) | copy-start | bytes 12292
  59.5 81.9 %copy-start.32 = (f32[1024]{0:T(1024)}, f32[1024]{0:T(1024)S(1)}, u32[]{:S(2)}) copy-start(f32[1024]{0:T(1024)S(1)} %convert_element_type.99) | copy-start | bytes 12292
  61.5 79.9 %copy-start.19 = (f32[1024]{0:T(1024)}, f32[1024]{0:T(1024)S(1)}, u32[]{:S(2)}) copy-start(f32[1024]{0:T(1024)S(1)} %broadcast_multiply_fusion.2) | copy-start | bytes 12292
  62.3 79.2 %copy-start.21 = (f32[1024]{0:T(1024)}, f32[1024]{0:T(1024)S(1)}, u32[]{:S(2)}) copy-start(f32[1024]{0:T(1024)S(1)} %add_rsqrt_fusion) | copy-start | bytes 12292
  63.3 49.7 %copy-start.23 = (f32[1024]{0:T(1024)}, f32[1024]{0:T(1024)S(1)}, u32[]{:S(2)}) copy-start(f32[1024]{0:T(1024)S(1)} %compare_convert_fusion) | copy-start | bytes 12292
  106.9 68.3 %copy-start.16 = (f32[1024,8]{0,1:T(8,128)}, f32[1024,8]{0,1:T(8,128)S(1)}, u32[]{:S(2)}) copy-start(f32[1024,8]{0,1:T(8,128)S(1)} %get-tuple-element.264) | copy-start | bytes 98308
  175.2 2.0 copy-start.9
  175.2 2.5 copy-start.10
  198.0 15.2 %copy-start = (bf16[1024,16,64]{0,2,1:T(8,128)(2,1)S(1)}, bf16[1024,16,64]{0,2,1:T(8,128)(2,1)}, u32[]{:S(2)}) copy-start(bf16[1024,16,64]{0,2,1:T(8,128)(2,1)} %get-tuple-element.425) | copy-start | bytes 6291460 | tf_op jit(solution)/shard_map/while
  246.0 15.3 %copy-start = (bf16[1024,16,64]{0,2,1:T(8,128)(2,1)S(1)}, bf16[1024,16,64]{0,2,1:T(8,128)(2,1)}, u32[]{:S(2)}) copy-start(bf16[1024,16,64]{0,2,1:T(8,128)(2,1)} %get-tuple-element.425) | copy-start | bytes 6291460 | tf_op jit(solution)/shard_map/while
  277.6 5.8 copy-start.14
  277.6 5.8 copy-start.24
  282.1 1.3 copy-start.12
  287.9 561.5 %reduce-scatter.5.cloned.1.call-start = ((), (), s32[]{:S(2)}) async-start(), calls=%async_computation.8 | async-start | bytes 12976128 | tf_op jit(solution)/shard_map/reduce_scatter | solution.py:256
  600.7 4.5 copy-start.11
  602.9 2.5 copy-start.17
  603.0 2.5 copy-start.18
  605.5 3.1 copy-start.3
  608.0 2.4 copy-start.2
  608.1 2.4 copy-start.20
  608.1 2.4 copy-start.22
  608.1 2.4 copy-start.28
  608.1 2.4 copy-start.33
  608.3 1.3 copy-start.5
  608.6 1.8 copy-start.7
  622.2 14.5 %copy-start.26 = (f32[32,1,128]{2,1,0:T(1,128)S(1)}, f32[32,1,128]{2,1,0:T(1,128)}, u32[]{:S(2)}) copy-start(f32[32,1,128]{2,1,0:T(1,128)} %convert_element_type.121) | copy-start | bytes 49156
  622.2 14.5 %copy-start.30 = (f32[1024]{0:T(1024)S(1)}, f32[1024]{0:T(1024)}, u32[]{:S(2)}) copy-start(f32[1024]{0:T(1024)} %convert_element_type.106) | copy-start | bytes 12292
  622.2 14.5 %copy-start.31 = (f32[1024]{0:T(1024)S(1)}, f32[1024]{0:T(1024)}, u32[]{:S(2)}) copy-start(f32[1024]{0:T(1024)} %convert_element_type.107) | copy-start | bytes 12292
  622.2 341.0 %reduce-scatter.9.cloned.1.call-start = ((), (), s32[]{:S(2)}) async-start(), calls=%async_computation.10 | async-start | bytes 17301504 | tf_op jit(solution)/shard_map/reduce_scatter | solution.py:257
  636.7 51.3 %copy-start.25 = (f32[1024]{0:T(1024)S(1)}, f32[1024]{0:T(1024)}, u32[]{:S(2)}) copy-start(f32[1024]{0:T(1024)} %copy-done.23) | copy-start | bytes 12292
  727.8 423.2 %reduce-scatter.11.cloned.1.call-start = ((), (), s32[]{:S(2)}) async-start(), calls=%async_computation.11 | async-start | bytes 17301504 | tf_op jit(solution)/shard_map/reduce_scatter | solution.py:265
  744.2 0.7 copy-start.35
  744.2 0.7 copy-start.34
  744.3 5.9 copy-start.13
  744.3 5.9 copy-start.37
  750.2 4.5 copy-start.4
  750.2 4.5 copy-start.6
  750.2 4.5 copy-start.8
  754.6 9.6 copy-start.29
  764.2 15.5 %copy-start.15 = (bf16[1024,1024]{1,0:T(8,128)(2,1)S(1)}, bf16[1024,1024]{1,0:T(8,128)(2,1)}, u32[]{:S(2)}) copy-start(bf16[1024,1024]{1,0:T(8,128)(2,1)} %param.21) | copy-start | bytes 6291460
  830.3 320.7 %copy-start.39 = (f32[32]{0:T(128)}, f32[32]{0:T(128)S(1)}, u32[]{:S(2)}) copy-start(f32[32]{0:T(128)S(1)} %dynamic-slice.1) | copy-start | bytes 388
Sparse Core Ops, SparseCore 0:
  10.9 59.3 all-gather.7
  73.1 68.2 all-gather.5
  144.9 75.9 all-gather.11
  223.6 76.1 all-gather.9
  302.5 139.5 reduce-scatter.6
  622.3 154.6 reduce-scatter.4
  780.0 183.1 reduce-scatter.8
  966.2 184.7 reduce-scatter.10
where the time goes:
time: 1170 us; the launch traced here: 1160 us
  matrix products  406 us (35%)
  waiting for transfers between devices  332 us (28%)
  local copies, waits for them, and re-layouts  157 us (13%)
  blocking collectives  130 us (11%)
  other arithmetic  110 us (9%)
  between operations  15.6 us (1%)
    reduce_scatter x1, waiting for transfers between devices, per_device(): lax.psum_scatter(down_weight_grad, 'dp', scatter_dimension=0, tiled=True)  188 us
    reduce_scatter x1, waiting for transfers between devices, per_device(): lax.psum_scatter(up_weight_grad, 'dp', scatter_dimension=0, tiled=True)  114 us
    unnamed x2, blocking collectives  89.4 us
    dynamic_update_slice x4, local copies, waits for them, and re-layouts, attention_forward(): lax.map(one_block, jnp.arange(rows // QBLOCK, dtype=jnp.int32))  83.3 us
    dot_general x4, matrix products, block_scores(): jnp.einsum('qhd,khd->hqk', block_query, keys, preferred_element_type=jnp....  60.9 us
    convert_element_type x2, other arithmetic, one_block(): score_grad = (probs * (prob_grad - inner)).astype(jnp.bfloat16)  55.8 us
    dot_general x4, matrix products, times_transposed(): lax.dot_general(left, right, (((1,), (1,)), ((), ())), preferred_element_...  55.6 us
    dot_general x2, matrix products, one_block(): jnp.einsum('qhd,khd->hqk', block_grad, values, preferred_element_type=jnp...  51.9 us
  transfers between devices with their start and end apart: 8, of which 3 were waited for; matrix products, arithmetic and copies ran while one was open for 58% of the time, Pallas kernels for 0%

commit v1 on v0

v1 whole, which is shorter than its diff:
```python
import jax
import jax.numpy as jnp
from jax import lax
from jax.experimental import pallas as pl
from jax.experimental.pallas import tpu as pltpu
from jax.sharding import PartitionSpec as P

D = 1024
HEADS = 16
HEAD = 64
FF = 4096
ROT = 16
QB = 256
PAIR = 128
REACH = 2
EPS = 1e-05
MASKED = -1e30


def layout(lengths, live_count, rows):
    ends = jnp.cumsum(lengths)
    starts = ends - lengths
    places = jnp.arange(rows, dtype=jnp.int32)
    segment = jnp.sum((places[:, None] >= ends[None, :]).astype(jnp.int32), axis=1)
    choose = segment[:, None] == jnp.arange(lengths.shape[0], dtype=jnp.int32)[None, :]
    offset = jnp.sum(jnp.where(choose, starts[None, :], 0), axis=1)
    live = (segment < live_count).astype(jnp.float32)
    return (offset, places - offset, live)


def rotary_lanes(positions):
    half = ROT // 2
    freqs = 10000.0 ** (-(2.0 * jnp.arange(half, dtype=jnp.float32)) / ROT)
    angles = positions.astype(jnp.float32)[:, None] * freqs[None, :]
    cosine, sine = jnp.cos(angles), jnp.sin(angles)
    rows = positions.shape[0]
    rest = HEAD - ROT
    turn = jnp.concatenate([cosine, cosine, jnp.ones((rows, rest), jnp.float32)], axis=1)
    cross = jnp.concatenate([-sine, sine, jnp.zeros((rows, rest), jnp.float32)], axis=1)
    return jnp.tile(turn, (1, PAIR // HEAD)), jnp.tile(cross, (1, PAIR // HEAD))


def outer_sum(left, right, kind=jnp.float32):
    return lax.dot_general(
        left, right, (((0,), (0,)), ((), ())), preferred_element_type=jnp.float32
    ).astype(kind)


def times_transposed(left, right):
    return lax.dot_general(
        left, right, (((1,), (1,)), ((), ())), preferred_element_type=jnp.float32
    )


def exchange(values):
    half = ROT // 2
    lane = lax.broadcasted_iota(jnp.int32, values.shape, 1)
    ahead = pltpu.roll(values, PAIR - half, 1)
    behind = pltpu.roll(values, half, 1)
    return jnp.where((lane & (HEAD - 1)) < half, ahead, behind)


def attention_kernel(
    q_in, k_in, v_in, grad_in, turn_ref, cross_ref, start_ref,
    out_ref, dq_ref, dk_ref, dv_ref,
    mask, q_low, k_low, v_low, dk_sum, dv_sum,
):
    rows = q_in.shape[0]
    blocks = rows // QB
    scale = HEAD ** (-0.5)

    @pl.when(pl.program_id(0) == 0)
    def _():
        for i in range(blocks):
            low = max(0, i - REACH) * QB
            width = (i + 1) * QB - low
            key = low + lax.broadcasted_iota(jnp.int32, (width, QB), 0)
            query = i * QB + lax.broadcasted_iota(jnp.int32, (width, QB), 1)
            start = start_ref[:, i * QB : (i + 1) * QB]
            mask[i, :width, :] = jnp.where((key >= start) & (key <= query), 0.0, MASKED)

    turn, cross = turn_ref[...], cross_ref[...]
    query = q_in[...]
    q_low[...] = ((query * turn + exchange(query) * cross).astype(jnp.bfloat16) * scale).astype(jnp.bfloat16)
    keys = k_in[...]
    k_low[...] = (keys * turn + exchange(keys) * cross).astype(jnp.bfloat16)
    v_low[...] = v_in[...].astype(jnp.bfloat16)
    dk_sum[...] = jnp.zeros_like(dk_sum)
    dv_sum[...] = jnp.zeros_like(dv_sum)
    k_turned = k_low[...].T
    v_turned = v_low[...].T
    for i in range(blocks):
        low = max(0, i - REACH) * QB
        high = (i + 1) * QB
        outs, grads = [], []
        for h in range(PAIR // HEAD):
            lanes = slice(h * HEAD, (h + 1) * HEAD)
            q = q_low[i * QB : high, lanes]
            do = grad_in[i * QB : high, lanes]
            k = k_low[low:high, lanes]
            v = v_low[low:high, lanes]
            scores = times_transposed(k, q) + mask[i, : high - low, :]
            largest = jnp.max(scores, axis=0, keepdims=True)
            weights = jnp.exp(scores - largest)
            inverse = 1.0 / jnp.sum(weights, axis=0, keepdims=True)
            probs = weights * inverse
            probs_low = probs.astype(jnp.bfloat16)
            outs.append(
                jnp.dot(v_turned[lanes, low:high], probs_low, preferred_element_type=jnp.float32)
            )
            dv_sum[low:high, lanes] += jnp.dot(probs_low, do, preferred_element_type=jnp.float32)
            weighted = times_transposed(v, do)
            inner = jnp.sum(probs * weighted, axis=0, keepdims=True)
            slope = (probs * (weighted - inner)).astype(jnp.bfloat16)
            grads.append(
                jnp.dot(k_turned[lanes, low:high], slope, preferred_element_type=jnp.float32)
            )
            dk_sum[low:high, lanes] += jnp.dot(slope, q, preferred_element_type=jnp.float32)
        out_ref[i * QB : high, :] = jnp.concatenate(outs, axis=0).T.astype(jnp.bfloat16)
        dq = jnp.concatenate(grads, axis=0).T * scale
        dq = dq * turn[i * QB : high, :] - exchange(dq) * cross[i * QB : high, :]
        dq_ref[i * QB : high, :] = dq.astype(jnp.bfloat16)
    dk = dk_sum[...]
    dk_ref[...] = (dk * turn - exchange(dk) * cross).astype(jnp.bfloat16)
    dv_ref[...] = dv_sum[...].astype(jnp.bfloat16)


def attention(joined, grad_low, turn, cross, start):
    rows = joined.shape[0]
    steps = D // PAIR
    blocks = rows // QB
    reach = min(REACH + 1, blocks) * QB

    def part(group):
        return pl.BlockSpec((rows, PAIR), lambda s: (0, s + group * steps))

    whole = pl.BlockSpec((rows, PAIR), lambda s: (0, 0))
    low = jax.ShapeDtypeStruct((rows, D), jnp.bfloat16)
    return pl.pallas_call(
        attention_kernel,
        grid=(steps,),
        in_specs=[
            part(0), part(1), part(2), part(0), whole, whole,
            pl.BlockSpec((1, rows), lambda s: (0, 0)),
        ],
        out_specs=[part(0)] * 4,
        out_shape=[low] * 4,
        scratch_shapes=[
            pltpu.VMEM((blocks, reach, QB), jnp.float32),
            pltpu.VMEM((rows, PAIR), jnp.bfloat16),
            pltpu.VMEM((rows, PAIR), jnp.bfloat16),
            pltpu.VMEM((rows, PAIR), jnp.bfloat16),
            pltpu.VMEM((rows, PAIR), jnp.float32),
            pltpu.VMEM((rows, PAIR), jnp.float32),
        ],
        compiler_params=pltpu.CompilerParams(vmem_limit_bytes=48 * 1024 * 1024),
        cost_estimate=pl.CostEstimate(
            flops=12 * 9 * HEADS * QB * QB * 256,
            bytes_accessed=24 * 1024 * 1024,
            transcendentals=9 * HEADS * QB * QB,
        ),
    )(joined, joined, joined, grad_low, turn, cross, start)


def gather(shard):
    return lax.all_gather(shard, "dp", axis=0, tiled=False)


def scatter(full):
    return lax.psum_scatter(full, "dp", scatter_dimension=0, tiled=True)


def make(count):
    def per_device(
        tokens, cotangent, seq_lengths, live_seqs,
        qkv_weight, qkv_bias, out_weight, out_bias, up_weight, up_bias, down_weight, down_bias,
        attn_gain, attn_shift, mlp_gain, mlp_shift,
    ):
        rows = tokens.shape[0]
        start, positions, live = layout(seq_lengths[0], live_seqs[0], rows)
        turn, cross = rotary_lanes(positions)
        small = (up_bias, mlp_gain, mlp_shift, qkv_bias, out_bias, down_bias, attn_gain, attn_shift)
        sizes = [member.shape[0] for member in small]
        packed = jnp.concatenate(small)
        packed = jnp.pad(packed, (0, FF - packed.shape[0]))[None, :]
        up_all = gather(jnp.concatenate([up_weight, packed], axis=0))
        local = up_weight.shape[0]
        up_full = up_all[:, :local].reshape(count * local, FF)
        pieces, begin = [], 0
        for size in sizes:
            piece = up_all[:, local, begin : begin + size].reshape(count * size)
            pieces.append(piece.astype(jnp.float32))
            begin += size
        hidden_bias, mlp_scale, mlp_offset, joined_bias, attn_bias, mlp_bias, attn_scale, attn_offset = pieces
        down_full = gather(down_weight).reshape(FF, D)
        qkv_full = gather(qkv_weight).reshape(D, 3 * D)
        out_full = gather(out_weight).reshape(D, D)

        inputs = tokens.astype(jnp.float32)
        average = jnp.mean(inputs, axis=1, keepdims=True)
        centred = inputs - average
        variance = jnp.mean(centred * centred, axis=1, keepdims=True)
        inverse = lax.rsqrt(variance + EPS)
        normed = centred * inverse
        attn_in = (normed * attn_scale + attn_offset).astype(jnp.bfloat16)
        mlp_in = (normed * mlp_scale + mlp_offset).astype(jnp.bfloat16)
        out_low = cotangent * live[:, None].astype(jnp.bfloat16)
        out_grad = out_low.astype(jnp.float32)

        hidden_pre = jnp.dot(mlp_in, up_full, preferred_element_type=jnp.float32) + hidden_bias
        share = 0.5 * (1.0 + lax.erf(hidden_pre * (0.5**0.5)))
        density = jnp.exp(-0.5 * hidden_pre * hidden_pre) * 0.3989422804014327
        hidden = (hidden_pre * share).astype(jnp.bfloat16)
        bend = (share + hidden_pre * density).astype(jnp.bfloat16)
        hidden, bend = lax.optimization_barrier((hidden, bend))
        down_grad = outer_sum(hidden, out_low, jnp.bfloat16)
        pre_grad = (times_transposed(out_low, down_full) * bend.astype(jnp.float32)).astype(jnp.bfloat16)
        up_grad = outer_sum(mlp_in, pre_grad, jnp.bfloat16)
        owned_down = scatter(down_grad)
        owned_up = scatter(up_grad)

        joined = jnp.dot(attn_in, qkv_full, preferred_element_type=jnp.float32) + joined_bias
        attended_grad = times_transposed(out_low, out_full).astype(jnp.bfloat16)
        attended, dq, dk, dv = attention(joined, attended_grad, turn, cross, start[None, :])
        joined_grad = jnp.concatenate([dq, dk, dv], axis=1)
        out_wgrad = outer_sum(attended, out_low, jnp.bfloat16)
        qkv_wgrad = outer_sum(attn_in, joined_grad, jnp.bfloat16)

        mlp_in_grad = times_transposed(pre_grad, up_full)
        attn_in_grad = times_transposed(joined_grad, qkv_full)
        vectors = (
            jnp.sum(joined_grad.astype(jnp.float32), axis=0),
            jnp.sum(out_grad, axis=0),
            jnp.sum(pre_grad.astype(jnp.float32), axis=0),
            jnp.sum(attn_in_grad * normed, axis=0),
            jnp.sum(attn_in_grad, axis=0),
            jnp.sum(mlp_in_grad * normed, axis=0),
            jnp.sum(mlp_in_grad, axis=0),
        )
        widths = [v.shape[0] // count for v in vectors]
        flat = jnp.concatenate([v.reshape(count, -1) for v in vectors], axis=1).astype(jnp.bfloat16)
        flat = jnp.pad(flat, ((0, 0), (0, D - flat.shape[1])))
        last = jnp.concatenate([out_wgrad.reshape(count, local, D), flat[:, None, :]], axis=1)
        owned_qkv = scatter(qkv_wgrad)
        owned_last = scatter(last)[0].astype(jnp.float32)
        owned_out = owned_last[:local]
        owned, begin = [], 0
        for width in widths:
            owned.append(owned_last[local, begin : begin + width])
            begin += width

        mixed = (
            inputs
            + jnp.dot(attended, out_full, preferred_element_type=jnp.float32)
            + jnp.dot(hidden, down_full, preferred_element_type=jnp.float32)
            + attn_bias
            + mlp_bias
        ).astype(jnp.bfloat16)
        normed_grad = attn_in_grad * attn_scale + mlp_in_grad * mlp_scale
        token_grad = (
            inverse
            * (
                normed_grad
                - jnp.mean(normed_grad, axis=1, keepdims=True)
                - normed * jnp.mean(normed_grad * normed, axis=1, keepdims=True)
            )
            + out_grad
        )
        return (
            mixed, token_grad,
            owned_qkv.astype(jnp.float32), owned[0],
            owned_out, owned[1],
            owned_up.astype(jnp.float32), owned[2],
            owned_down.astype(jnp.float32), owned[1],
            owned[3], owned[4], owned[5], owned[6],
        )

    return per_device


def solution(mesh):
    rows, flat = P("dp", None), P("dp")
    return jax.shard_map(
        make(mesh.shape["dp"]),
        mesh=mesh,
        in_specs=(rows, rows, rows, flat) + (rows, flat) * 4 + (flat,) * 4,
        out_specs=(rows, rows) + (rows, flat) * 4 + (flat,) * 4,
        check_vma=False,
    )
```

time: 1170 us -> 967 us (0.83)
  waiting for transfers between devices: 332 us -> 674 us
  matrix products: 406 us -> 150 us
  local copies, waits for them, and re-layouts: 157 us -> 26.8 us
  blocking collectives: 130 us -> 0 us
  other arithmetic: 110 us -> 27.1 us
  Pallas kernels: 0 us -> 68.7 us
    dot_general x18 -> x4, matrix products: 302 us -> 52.5 us  [the longest x1 20.3 us: per_device(): jnp.dot(mlp_in, up_full, preferred_element_type=jnp.float32) + hidden_bias]
    reduce_scatter x4, waiting for transfers between devices: 302 us -> 477 us  [scatter(): return lax.psum_scatter(full, 'dp', scatter_dimension=0, tiled=True)]
    all_gather x4, waiting for transfers between devices: 28.5 us -> 195 us  [gather(): return lax.all_gather(shard, 'dp', axis=0, tiled=False)]
    unnamed x2 -> x0, blocking collectives: 89.4 us -> none
    dynamic_update_slice x4 -> x0, local copies, waits for them, and re-layouts: 83.3 us -> none  [attention_forward(): lax.map(one_block, jnp.arange(rows // QBLOCK, dtype=jnp.int32))]
    pallas_call x0 -> x1, Pallas kernels: none -> 68.7 us  [attention(): pl.pallas_call(attention_kernel, grid=(steps,), in_specs=[part(0), part(1...]
    convert_element_type x12 -> x9, other arithmetic: 57.7 us -> 10.1 us  [the longest x3 3.87 us: per_device(): pieces.append(piece.astype(jnp.float32))]
    all_gather x1 -> x0, blocking collectives: 41 us -> none  [per_device(): lax.all_gather(up_bias, 'dp', axis=0, tiled=True)]
  transfers between devices with their start and end apart: 8 -> 8, of which waited for: 3 -> 7; matrix products, arithmetic and copies ran while one was open for 58% -> 17% of each run, Pallas kernels for 0% -> 7%
where the time goes in v1:
time: 967 us; the launch traced here: 962 us
  waiting for transfers between devices  674 us (70%)
  matrix products  150 us (16%)
  Pallas kernels  68.7 us (7%)
  other arithmetic  27.1 us (3%)
  local copies, waits for them, and re-layouts  26.8 us (3%)
  between operations  15.2 us (2%)
    reduce_scatter x4, waiting for transfers between devices, scatter(): return lax.psum_scatter(full, 'dp', scatter_dimension=0, tiled=True)  477 us
    all_gather x4, waiting for transfers between devices, gather(): return lax.all_gather(shard, 'dp', axis=0, tiled=False)  195 us
    pallas_call x1, Pallas kernels, attention(): pl.pallas_call(attention_kernel, grid=(steps,), in_specs=[part(0), part(1...  68.7 us
    dot_general x4, matrix products, times_transposed(): lax.dot_general(left, right, (((1,), (1,)), ((), ())), preferred_element_...  51 us
    dot_general x4, matrix products, outer_sum(): lax.dot_general(left, right, (((0,), (0,)), ((), ())), preferred_element_...  46.7 us
    dot_general x1, matrix products, per_device(): jnp.dot(mlp_in, up_full, preferred_element_type=jnp.float32) + hidden_bias  20.3 us
  transfers between devices with their start and end apart: 8, of which 7 were waited for; matrix products, arithmetic and copies ran while one was open for 17% of the time, Pallas kernels for 7%

profile of v1, /device:TPU:0, one launch (start us, length us, event | category | flops | bytes accessed | tf_op | source)
XLA Modules:
  0.0 962.2 jit_solution(7144505522950605121)
XLA Ops:
  7.2 0.7 all-gather.12.cloned.1.call-update
  8.0 5.4 concatenate.22
  13.4 1.7 maximum_bitcast_fusion
  15.2 0.7 all-gather.10.cloned.1.call-update
  15.9 0.5 all-gather.14.cloned.1.call-update
  17.3 0.8 reduce-window.4
  18.2 0.1 convert_reduce_fusion.1
  18.3 2.1 fusion.42
  20.3 0.7 reshape.196
  21.0 0.7 fusion.36
  21.7 0.1 select_reduce_fusion
  21.8 0.2 fusion.35
  22.0 0.1 maximum_maximum_fusion
  22.2 0.2 copy.36.turn_ref
  22.4 0.9 tile.20
  23.2 1.2 copy.37.cross_ref
  24.5 0.3 convert_reduce_fusion
  24.8 0.7 fusion.23
  25.5 44.5 %all-gather.12.cloned.1.call-done = bf16[1024,1024]{1,0:T(8,128)(2,1)} async-done(((bf16[32,1024]{1,0:T(8,128)(2,1)}), bf16[1024,1024]{1,0:T(8,128)(2,1)}) %all-gather.12.cloned.1.call-update) | async-done | bytes 2097168 | tf_op jit(solution)/shard_map/all_gather | solution.py:166
  70.0 5.9 convolution_convert_fusion.4.grad_in
  76.0 83.1 %all-gather.16.cloned.1.call-done = bf16[32,33,4096]{2,1,0:T(8,128)(2,1)} async-done(((bf16[1,33,4096]{2,1,0:T(8,128)(2,1)}), bf16[32,33,4096]{2,1,0:T(8,128)(2,1)}) %all-gather.16.cloned.1.call-update) | async-done | bytes 8650768 | tf_op jit(solution)/shard_map/all_gather | solution.py:166
  159.1 1.0 fusion.32
  160.2 2.0 fusion.31
  162.5 67.5 %all-gather.10.cloned.1.call-done = bf16[1024,3072]{1,0:T(8,128)(2,1)} async-done(((bf16[32,3072]{1,0:T(8,128)(2,1)}), bf16[1024,3072]{1,0:T(8,128)(2,1)}) %all-gather.10.cloned.1.call-update) | async-done | bytes 6291472 | tf_op jit(solution)/shard_map/all_gather | solution.py:166
  230.0 13.2 %broadcast_add_fusion.q_in.k_in.v_in = f32[1024,3072]{1,0:T(8,128)} fusion(f32[3072]{0:T(1024)S(1)} %reshape.204, bf16[1024,3072]{1,0:T(8,128)(2,1)} %all-gather.10.cloned.1.call-done, bf16[1024,1024]{1,0:T(8,128)(2,1)S(1)} %copy-done, f32[1024]{0:T(1024)S(1)} %reshape.203, f32[1024]{0:T(1024)S(1)} %reshape.202, f32[1024]{0:T(1024)S(1)} %add_rsqrt_fusion, ...), kind=kOutput, calls=%fused_computation.11 | convolution fusion | flops 6451888128 | bytes 21000192 | tf_op jit(solution)/shard_map/dot_general | solution.py:222
  243.2 68.7 %shard_map.263 = (bf16[1024,1024]{1,0:T(8,128)(2,1)S(1)}, bf16[1024,1024]{1,0:T(8,128)(2,1)S(1)}, bf16[1024,1024]{1,0:T(8,128)(2,1)}, bf16[1024,1024]{1,0:T(8,128)(2,1)}) custom-call(f32[1024,3072]{1,0:T(8,128)} %broadcast_add_fusion.q_in.k_in.v_in, f32[1024,3072]{1,0:T(8,128)} %broadcast_add_fusion.q_in.k_in.v_in, ...), custom_call_target="tpu_custom_call" | custom-call | flops 28991029248 | bytes 25165824 | tf_op jit(solution)/shard_map/pallas_call | solution.py:139
  312.0 1.5 constant_dynamic-update-slice_fusion.2
  313.5 0.8 copy-done.7
  314.3 1.7 constant_dynamic-update-slice_fusion.1
  316.0 1.6 constant_dynamic-update-slice_fusion
  317.5 3.7 reduce
  321.2 0.1 reshape.195
  321.3 8.0 slice.77
  329.3 0.8 slice_convert_fusion.2
  330.2 20.3 %fusion.4 = (bf16[1024,4096]{1,0:T(8,128)(2,1)}, bf16[1024,4096]{1,0:T(8,128)(2,1)}) fusion(f32[4096]{0:T(1024)S(1)} %bitcast.61, bf16[1024,4096]{1,0:T(8,128)(2,1)} %bitcast.56, bf16[1024,1024]{1,0:T(8,128)(2,1)S(1)} %copy-done.1, f32[1024]{0:T(1024)S(1)} %reshape.206, f32[1024]{0:T(1024)S(1)} %reshape.205, f32[1024]{0:T(1024)S(1)} %add_rsqrt_fusion, ...), kind=kOutput, calls=%fused_computation.5 | convolution fusion | flops 8646557696 | bytes 27295744 | tf_op jit(solution)/shard_map/dot_general | solution.py:210
  350.5 3.8 convolution_convert_fusion.3
  354.3 12.0 %fusion.49 = f32[1024,1024]{1,0:T(8,128)} fusion(bf16[1024,3072]{1,0:T(8,128)(2,1)} %constant_dynamic-update-slice_fusion, bf16[1024,3072]{1,0:T(8,128)(2,1)} %all-gather.10.cloned.1.call-done), kind=kOutput, calls=%fused_computation.99 | convolution fusion | flops 6442450944 | bytes 16777216 | tf_op jit(solution)/shard_map/dot_general | solution.py:50
  366.3 15.6 %fusion.47 = (bf16[4096]{0:T(1024)(128)(2,1)S(1)}, bf16[1024,4096]{1,0:T(8,128)(2,1)}) fusion(bf16[1024,4096]{1,0:T(8,128)(2,1)} %get-tuple-element.25, bf16[4096,1024]{1,0:T(8,128)(2,1)} %all-gather.14.cloned.1.call-done, bf16[1024,1024]{1,0:T(8,128)(2,1)} %param.17, bf16[1024]{0:T(1024)(128)(2,1)S(1)} %convert_convert_fusion), kind=kOutput, calls=%fused_computation.97 | convolution fusion | flops 8607756288 | bytes 27273216 | tf_op jit(solution)/shard_map/dot_general | solution.py:50
  381.9 17.5 %fusion.43 = (bf16[1024]{0:T(1024)(128)(2,1)S(1)}, bf16[1024]{0:T(1024)(128)(2,1)S(1)}, f32[1024]{0:T(1024)S(1)}, f32[1024]{0:T(1024)S(1)}, f32[1024,1024]{1,0:T...) fusion(f32[1024]{0:T(1024)S(1)} %add_rsqrt_fusion, f32[1024]{0:T(1024)S(1)} %broadcast_multiply_fusion.3, ...), kind=kOutput, calls=%fused_computation.93 | convolution fusion | flops 8605657088 | bytes 27295744 | tf_op jit(solution)/shard_map/dot_general | solution.py:50
  399.4 0.1 reshape.201
  399.5 0.1 reshape.200
  399.7 0.1 concatenate.27
  399.9 0.1 copy.38
  400.0 3.6 pad_maximum_fusion
  403.6 12.2 %convolution_convert_fusion.2 = bf16[1024,3072]{1,0:T(8,128)(2,1)} fusion(bf16[1024,3072]{1,0:T(8,128)(2,1)} %constant_dynamic-update-slice_fusion, bf16[1024,1024]{1,0:T(8,128)(2,1)} %param.16, f32[1024]{0:T(1024)S(1)} %reshape.203, f32[1024]{0:T(1024)S(1)} %reshape.202, f32[1024]{0:T(1024)S(1)} %add_rsqrt_fusion, f32[1024]{0:T(1024)S(1)} %broadcast_multiply_fusion.3), kind=kOutput, calls=%fused_computation.15 | convolution fusion | flops 6451888128 | bytes 14696448 | tf_op jit(solution)/shard_map/dot_general | solution.py:44
  415.9 15.5 %convolution_convert_fusion.1 = bf16[1024,4096]{1,0:T(8,128)(2,1)} fusion(bf16[1024,4096]{1,0:T(8,128)(2,1)} %get-tuple-element.57, bf16[1024,1024]{1,0:T(8,128)(2,1)} %param.16, f32[1024]{0:T(1024)S(1)} %reshape.206, f32[1024]{0:T(1024)S(1)} %reshape.205, f32[1024]{0:T(1024)S(1)} %add_rsqrt_fusion, f32[1024]{0:T(1024)S(1)} %broadcast_multiply_fusion.3), kind=kOutput, calls=%fused_computation.10 | convolution fusion | flops 8600420352 | bytes 18890752 | tf_op jit(solution)/shard_map/dot_general | solution.py:44
  431.4 15.3 %convolution_convert_fusion = bf16[4096,1024]{1,0:T(8,128)(2,1)} fusion(bf16[1024,4096]{1,0:T(8,128)(2,1)} %get-tuple-element.21, bf16[1024,1024]{1,0:T(8,128)(2,1)} %param.17, bf16[1024]{0:T(1024)(128)(2,1)S(1)} %convert_convert_fusion), kind=kOutput, calls=%fused_computation.9 | convolution fusion | flops 8595177472 | bytes 18876416 | tf_op jit(solution)/shard_map/dot_general | solution.py:44
  446.7 0.7 copy-done.9
  447.6 4.1 fusion.48
  451.8 2.9 fusion.20
  454.7 14.9 %fusion.27 = bf16[1024,1024]{1,0:T(8,128)(2,1)} fusion(f32[1024,1024]{1,0:T(8,128)S(1)} %fusion.48, bf16[1024,1024]{1,0:T(8,128)(2,1)S(1)} %copy-done.2, f32[1024]{0:T(1024)S(1)} %reshape.209, f32[1024]{0:T(1024)S(1)} %reshape.208, bf16[1024,4096]{1,0:T(8,128)(2,1)} %get-tuple-element.21, bf16[4096,1024]{1,0:T(8,128)(2,1)} %all-gather.14.cloned.1.call-done), kind=kOutput, calls=%fused_computation.38 | convolution fusion | flops 8596226048 | bytes 25174016 | tf_op jit(solution)/shard_map/dot_general | solution.py:255
  469.6 70.2 %reduce-scatter.7.cloned.1.call-done = bf16[1,33,1024]{2,1,0:T(8,128)(2,1)} async-done(((bf16[32,33,1024]{2,1,0:T(8,128)(2,1)}), bf16[1,33,1024]{2,1,0:T(8,128)(2,1)}) %reduce-scatter.7.cloned.1.call-update) | async-done | bytes 67600 | tf_op jit(solution)/shard_map/reduce_scatter | solution.py:170
  539.8 0.9 fusion.46
  540.7 0.6 slice_bitcast_fusion.1
  541.3 0.5 slice_bitcast_fusion.5
  541.9 0.5 slice_bitcast_fusion.7
  542.4 0.7 slice_bitcast_fusion
  543.0 112.6 %reduce-scatter.5.cloned.1.call-done = bf16[32,3072]{1,0:T(8,128)(2,1)} async-done(((bf16[1024,3072]{1,0:T(8,128)(2,1)}), bf16[32,3072]{1,0:T(8,128)(2,1)}) %reduce-scatter.5.cloned.1.call-update) | async-done | bytes 196624 | tf_op jit(solution)/shard_map/reduce_scatter | solution.py:170
  655.6 1.7 convert_element_type.204
  657.3 148.6 %reduce-scatter.9.cloned.1.call-done = bf16[32,4096]{1,0:T(8,128)(2,1)} async-done(((bf16[1024,4096]{1,0:T(8,128)(2,1)}), bf16[32,4096]{1,0:T(8,128)(2,1)}) %reduce-scatter.9.cloned.1.call-update) | async-done | bytes 262160 | tf_op jit(solution)/shard_map/reduce_scatter | solution.py:170
  806.0 1.8 convert_element_type.211
  807.7 145.1 %reduce-scatter.11.cloned.1.call-done = bf16[128,1024]{1,0:T(8,128)(2,1)} async-done(((bf16[4096,1024]{1,0:T(8,128)(2,1)}), bf16[128,1024]{1,0:T(8,128)(2,1)}) %reduce-scatter.11.cloned.1.call-update) | async-done | bytes 262160 | tf_op jit(solution)/shard_map/reduce_scatter | solution.py:170
  952.9 1.8 convert_element_type.213
  954.7 0.5 copy.43
  (60 shorter events, 1.4 us)
Async XLA Ops:
  7.2 17.3 %copy-start = (bf16[1024,1024]{1,0:T(8,128)(2,1)S(1)}, bf16[1024,1024]{1,0:T(8,128)(2,1)}, u32[]{:S(2)}) copy-start(bf16[1024,1024]{1,0:T(8,128)(2,1)} %param.16) | copy-start | bytes 6291460
  7.2 62.8 %all-gather.12.cloned.1.call-start = ((), (), s32[]{:S(2)}) async-start(), calls=%async_computation.9 | async-start | bytes 2162688 | tf_op jit(solution)/shard_map/all_gather | solution.py:166
  7.9 151.2 %all-gather.16.cloned.1.call-start = ((), (), s32[]{:S(2)}) async-start(), calls=%async_computation.11 | async-start | bytes 10813440 | tf_op jit(solution)/shard_map/all_gather | solution.py:166
  15.2 214.8 %all-gather.10.cloned.1.call-start = ((), (), s32[]{:S(2)}) async-start(), calls=%async_computation.8 | async-start | bytes 6488064 | tf_op jit(solution)/shard_map/all_gather | solution.py:166
  15.9 350.4 %all-gather.14.cloned.1.call-start = ((), (), s32[]{:S(2)}) async-start(), calls=%async_computation.10 | async-start | bytes 8650752 | tf_op jit(solution)/shard_map/all_gather | solution.py:166
  16.5 523.4 %reduce-scatter.7.cloned.1.call-start = ((), (), s32[]{:S(2)}) async-start(), calls=%async_computation.5 | async-start | bytes 2703360 | tf_op jit(solution)/shard_map/reduce_scatter | solution.py:170
  311.9 2.4 copy-start.7
  311.9 4.0 copy-start.6
  321.3 8.8 copy-start.1
  330.2 20.3 %copy-start.3 = (bf16[1024,1024]{1,0:T(8,128)(2,1)S(1)}, bf16[1024,1024]{1,0:T(8,128)(2,1)}, u32[]{:S(2)}) copy-start(bf16[1024,1024]{1,0:T(8,128)(2,1)} %param.17) | copy-start | bytes 6291460
  381.9 17.9 %copy-start.10 = (bf16[32,32]{1,0:T(8,128)(2,1)S(1)}, bf16[32,32]{1,0:T(8,128)(2,1)}, u32[]{:S(2)}) copy-start(bf16[32,32]{1,0:T(8,128)(2,1)} %reshape.196) | copy-start | bytes 6148
  403.5 252.1 %reduce-scatter.5.cloned.1.call-start = ((), (), s32[]{:S(2)}) async-start(), calls=%async_computation.4 | async-start | bytes 6488064 | tf_op jit(solution)/shard_map/reduce_scatter | solution.py:170
  415.8 390.1 %reduce-scatter.9.cloned.1.call-start = ((), (), s32[]{:S(2)}) async-start(), calls=%async_computation.6 | async-start | bytes 8650752 | tf_op jit(solution)/shard_map/reduce_scatter | solution.py:170
  431.4 521.5 %reduce-scatter.11.cloned.1.call-start = ((), (), s32[]{:S(2)}) async-start(), calls=%async_computation.7 | async-start | bytes 8650752 | tf_op jit(solution)/shard_map/reduce_scatter | solution.py:170
  446.7 0.7 copy-start.9
  446.7 0.8 copy-start.8
  447.6 4.1 copy-start.2
  447.6 4.1 copy-start.4
  447.6 4.2 copy-start.5
  541.3 413.8 %copy-start.11 = (f32[32]{0:T(128)}, f32[32]{0:T(128)S(1)}, u32[]{:S(2)}) copy-start(f32[32]{0:T(128)S(1)} %get-tuple-element.83) | copy-start | bytes 388
Sparse Core Ops, SparseCore 0:
  10.9 59.1 all-gather.11
  73.4 85.5 all-gather.15
  162.0 68.0 all-gather.9
  232.7 75.9 all-gather.13
  403.7 136.1 reduce-scatter.6
  545.3 110.2 reduce-scatter.4
  658.0 147.8 reduce-scatter.8
  808.3 144.4 reduce-scatter.10
